TPU v7x, 256 devices: a whole 4x4x8 slice. The times are simulated.
256 devices in a mesh: gx: 8 (over x, core), gy: 8 (over z_hi, y), pa: 4 (over z_lo).
Axes of the slice: x: 4, y: 4, z: 8 (z_hi: 2, z_lo: 4; z = z_hi * 4 + z_lo), core: 2. Of those that a mesh axis runs over, the one named last changes fastest.
Arguments:
- mixing_ratios: float32 [120, 1, 32, 1024], P(None, None, 'gx', 'gy'), may hold values from 0.1 to 2
- derivative_field: float32 [120, 16, 1, 32, 1024], P(None, 'pa', None, 'gx', 'gy'), may hold values from -6 to 6
- thermal_kelvin: float32 [1, 32, 1024], P(None, 'gx', 'gy'), may hold values from 260 to 310
- eastward_cfl_ratio: float32 [1, 32, 1024], P(None, 'gx', 'gy'), may hold values from -0.3 to 0.3
- northward_cfl_ratio: float32 [1, 32, 1024], P(None, 'gx', 'gy'), may hold values from -0.3 to 0.3
- lateral_mixing_coef: float32 [1, 32, 1024], P(None, 'gx', 'gy'), may hold values from 0.02 to 0.08
- prefactor_times_dt: float32 [360], replicated, may hold values from 0.01 to 0.1
- barrier_kelvin: float32 [360], replicated, may hold values from 0 to 2000
- input_compound_pair: int32 [360, 2], replicated, may hold values from 0 to 119
- output_yield_matrix: int32 [120, 360], replicated, may hold values from 0 to 2
- partition_solver_matrices: bfloat16 [120, 120, 1, 32, 1024], P(None, None, None, ('gx', 'pa'), 'gy'), may hold values from -2 to 2
- ground_flux_per_tick: float32 [32, 1024], P('gx', 'gy'), may hold values from 0.5 to 2
- cell_zone_label: int32 [32, 1024], P('gx', 'gy'), may hold values from 0 to 7
- knob_target_compound: int32 [16], P('pa'), may hold values from 0 to 119
- knob_zone: int32 [16], P('pa'), may hold values from 0 to 7
Outputs:
- new_sens: float32 [120, 16, 1, 32, 1024], P(None, 'pa', None, 'gx', 'gy')
All inputs are finite; a program needn't handle non-finite values.
Results may differ from a plain program's by a relative error of at most 0.0021.
Values may be sent and summed in bfloat16 or wider, within the bound.
A program may use at most 128 MiB of HBM per device.

v0:
```python
import jax
import jax.numpy as jnp
from jax import lax
from jax.sharding import PartitionSpec as P

NSUB = 2


def extended(shard, sides, width):
    for axis, dim in sides:
        devices, length = (lax.axis_size(axis), shard.shape[dim])
        up = [(i, (i + 1) % devices) for i in range(devices - 1)]
        down = [(j, i) for i, j in up]
        last = lax.slice_in_dim(shard, length - width, length, axis=dim)
        initial = lax.slice_in_dim(shard, 0, width, axis=dim)
        before = lax.ppermute(last, axis, up)
        after = lax.ppermute(initial, axis, down)
        shard = jnp.concatenate([before, shard, after], axis=dim)
    return shard


def stencil(padded, eastward_cfl_ratio, northward_cfl_ratio, lateral_mixing_coef):
    center = padded[..., 1:-1, 1:-1]
    x_minus = padded[..., :-2, 1:-1]
    x_plus = padded[..., 2:, 1:-1]
    y_minus = padded[..., 1:-1, :-2]
    y_plus = padded[..., 1:-1, 2:]
    along_x = jnp.maximum(eastward_cfl_ratio, 0.0) * (center - x_minus) + jnp.minimum(
        eastward_cfl_ratio, 0.0
    ) * (x_plus - center)
    along_y = jnp.maximum(northward_cfl_ratio, 0.0) * (center - y_minus) + jnp.minimum(
        northward_cfl_ratio, 0.0
    ) * (y_plus - center)
    return (
        center
        - along_x
        - along_y
        + lateral_mixing_coef * (x_plus + x_minus + y_plus + y_minus - 4.0 * center)
    )


def advect(fields, eastward_cfl_ratio, northward_cfl_ratio, lateral_mixing_coef):
    for substep in range(NSUB):
        padded = extended(fields, (("gx", 3), ("gy", 4)), 1)
        fields = stencil(padded, eastward_cfl_ratio, northward_cfl_ratio, lateral_mixing_coef)
    return fields


def coefficients(conc_rows, scratch_lines, prefactor_times_dt, barrier_kelvin, input_compound_pair):
    rate_const = prefactor_times_dt[:, None, None, None] * jnp.exp(
        -barrier_kelvin[:, None, None, None] * (1.0 / scratch_lines[None] - 1.0 / 298.0)
    )
    first_coef = rate_const * jnp.take(conc_rows, input_compound_pair[:, 1], axis=0)
    second = rate_const * jnp.take(conc_rows, input_compound_pair[:, 0], axis=0)
    return jnp.stack([first_coef, second]).astype(jnp.bfloat16)


def net_matrix(output_yield_matrix, input_compound_pair):
    species_ids = jnp.arange(output_yield_matrix.shape[0], dtype=jnp.int32)[:, None]
    consumed = (species_ids == input_compound_pair[None, :, 0]).astype(jnp.int32) + (
        species_ids == input_compound_pair[None, :, 1]
    ).astype(jnp.int32)
    return (output_yield_matrix - consumed).astype(jnp.bfloat16)


def emission_source(species, levels, knob_target_compound, knob_zone, zone_rows, base_rows):
    hit_species = (
        jnp.arange(species, dtype=jnp.int32)[:, None] == knob_target_compound[None, :]
    ).astype(jnp.float32)
    hit_zone = (zone_rows[None] == knob_zone[:, None, None]).astype(jnp.float32)
    surface = (jnp.arange(levels, dtype=jnp.int32) == 0).astype(jnp.float32)
    return (
        hit_species[:, :, None, None, None]
        * hit_zone[None, :, None]
        * surface[None, None, :, None, None]
        * base_rows[None, None, None]
    )


def apply_jacobian(tangent, coeffs, net_stoich, input_compound_pair):
    left_sens = jnp.take(tangent, input_compound_pair[:, 0], axis=0)
    right_sens = jnp.take(tangent, input_compound_pair[:, 1], axis=0)
    flux_bf = (coeffs[0][:, None] * left_sens + coeffs[1][:, None] * right_sens).astype(
        jnp.bfloat16
    )
    reaction_count = flux_bf.shape[0]
    product = jnp.dot(
        net_stoich, flux_bf.reshape(reaction_count, -1), preferred_element_type=jnp.float32
    )
    return product.reshape(tangent.shape)


def apply_inverse(rhs_bf, partition_solver_matrices):
    at_owner = lax.all_to_all(rhs_bf, "pa", split_axis=3, concat_axis=1, tiled=True)
    result = jnp.einsum(
        "ijlxy,jplxy->iplxy",
        partition_solver_matrices,
        at_owner,
        preferred_element_type=jnp.float32,
    )
    return lax.all_to_all(result, "pa", split_axis=1, concat_axis=3, tiled=True)


def shards(
    mixing_ratios,
    derivative_field,
    thermal_kelvin,
    eastward_cfl_ratio,
    northward_cfl_ratio,
    lateral_mixing_coef,
    prefactor_times_dt,
    barrier_kelvin,
    input_compound_pair,
    output_yield_matrix,
    partition_solver_matrices,
    ground_flux_per_tick,
    cell_zone_label,
    knob_target_compound,
    knob_zone,
):
    fields = jnp.concatenate([mixing_ratios[:, None], derivative_field], axis=1)
    fields = advect(fields, eastward_cfl_ratio, northward_cfl_ratio, lateral_mixing_coef)
    moved_conc = fields[:, 0]
    moved_sens = fields[:, 1:]
    height_total = mixing_ratios.shape[2] // lax.axis_size("pa")
    offset_begin = lax.axis_index("pa") * height_total
    conc_rows = lax.dynamic_slice_in_dim(moved_conc, offset_begin, height_total, 2)
    scratch_lines = lax.dynamic_slice_in_dim(thermal_kelvin, offset_begin, height_total, 1)
    coeffs = lax.all_gather(
        coefficients(
            conc_rows, scratch_lines, prefactor_times_dt, barrier_kelvin, input_compound_pair
        ),
        "pa",
        axis=3,
        tiled=True,
    )
    net_stoich = net_matrix(output_yield_matrix, input_compound_pair)
    source = emission_source(
        mixing_ratios.shape[0],
        mixing_ratios.shape[1],
        knob_target_compound,
        knob_zone,
        cell_zone_label,
        ground_flux_per_tick,
    )
    rhs_one = (apply_jacobian(moved_sens, coeffs, net_stoich, input_compound_pair) + source).astype(
        jnp.bfloat16
    )
    k_one = apply_inverse(rhs_one, partition_solver_matrices)
    rhs_two = (
        apply_jacobian(moved_sens + k_one, coeffs, net_stoich, input_compound_pair)
        + source
        - 2.0 * k_one
    ).astype(jnp.bfloat16)
    k_two = apply_inverse(rhs_two, partition_solver_matrices)
    return moved_sens + 1.5 * k_one + 0.5 * k_two


def solution(mesh):
    in_specs = (
        P(None, None, "gx", "gy"),
        P(None, "pa", None, "gx", "gy"),
        P(None, "gx", "gy"),
        P(None, "gx", "gy"),
        P(None, "gx", "gy"),
        P(None, "gx", "gy"),
        P(),
        P(),
        P(),
        P(),
        P(None, None, None, ("gx", "pa"), "gy"),
        P("gx", "gy"),
        P("gx", "gy"),
        P("pa"),
        P("pa"),
    )
    out_specs = P(None, "pa", None, "gx", "gy")
    return jax.shard_map(shards, mesh=mesh, in_specs=in_specs, out_specs=out_specs, check_vma=False)
```

profile of v0, /device:TPU:130, one launch (start us, length us, event | category | flops | bytes accessed | tf_op | source)
XLA Modules:
  0.0 244.4 jit_solution(13466022354709991660)
XLA Ops:
  4.5 3.6 %collective-permute-start.1 = (f32[120,5,1,1,128]{4,0,3,1,2:T(8,128)S(1)}, f32[120,5,1,1,128]{4,0,3,1,2:T(8,128)S(1)}, u32[]{:S(2)}, u32[]{:S(2)}) collective-permute-start(f32[120,5,1,1,128]{4,0,3,1,2:T(8,128)S(1)} %get-tuple-element.16), channel_id=1, source_target_pairs={{32,0},{64,32},{96,64},{128,96},{160,128},{192,160},{224,192},{33,... | collective-permute-start | bytes 921608 | tf_op jit(solution)/shard_map/ppermute | solution.py:17
  17.8 3.1 %collective-permute-start.3 = (f32[120,5,1,6,1]{0,4,3,2,1:T(1,128)S(1)}, f32[120,5,1,6,1]{0,4,3,2,1:T(1,128)S(1)}, u32[]{:S(2)}, u32[]{:S(2)}) collective-permute-start(f32[120,5,1,6,1]{0,4,3,2,1:T(1,128)S(1)} %copy.46), channel_id=1, source_target_pairs={{4,0},{8,4},{12,8},{16,12},{20,16},{24,20},{28,24},{5,1},{9,5},{13... | collective-permute-start | bytes 43208 | tf_op jit(solution)/shard_map/ppermute | solution.py:17
  23.7 8.9 %collective-permute-done.2 = f32[120,5,1,6,1]{0,4,3,2,1:T(1,128)S(1)} collective-permute-done((f32[120,5,1,6,1]{0,4,3,2,1:T(1,128)S(1)}, f32[120,5,1,6,1]{0,4,3,2,1:T(1,128)S(1)}, u32[]{:S(2)}, u32[]{:S(2)}) %collective-permute-start.2) | collective-permute-done | bytes 14432 | tf_op jit(solution)/shard_map/ppermute | solution.py:16
  36.3 3.5 %multiply_add_fusion = f32[120,5,1,4,128]{4,0,3,1,2:T(8,128)S(1)} fusion(f32[120,5,1,6,1]{4,0,3,1,2:T(8,128)} %copy.47, f32[120,5,1,1,128]{4,0,3,1,2:T(8,128)S(1)} %copy-done.5, f32[120,4,1,4,128]{4,0,3,1,2:T(8,128)S(1)} %copy.43, f32[120,1,1,4,128]{4,0,3,1,2:T(8,128)S(1)} %bitcast.157, f32[120,5,1,1,128]{4,0,3,1,2:T(8,128)S(1)} %collective-permute-done, ...), kind=kLoop, calls=%fused_computation.69 | loop fusion | flops 9830400 | bytes 3111040 | tf_op jit(solution)/shard_map/add | solution.py:35
  42.1 3.3 %collective-permute-start.5 = (f32[120,5,1,1,128]{4,0,3,1,2:T(8,128)S(1)}, f32[120,5,1,1,128]{4,0,3,1,2:T(8,128)S(1)}, u32[]{:S(2)}, u32[]{:S(2)}) collective-permute-start(f32[120,5,1,1,128]{4,0,3,1,2:T(8,128)S(1)} %get-tuple-element.14), channel_id=1, source_target_pairs={{32,0},{64,32},{96,64},{128,96},{160,128},{192,160},{224,192},{33,... | collective-permute-start | bytes 921608 | tf_op jit(solution)/shard_map/ppermute | solution.py:17
  58.3 3.9 %collective-permute-start.6 = (f32[120,5,1,6,1]{0,4,3,2,1:T(1,128)S(1)}, f32[120,5,1,6,1]{0,4,3,2,1:T(1,128)S(1)}, u32[]{:S(2)}, u32[]{:S(2)}) collective-permute-start(f32[120,5,1,6,1]{0,4,3,2,1:T(1,128)S(1)} %copy.48), channel_id=1, source_target_pairs={{0,4},{4,8},{8,12},{12,16},{16,20},{20,24},{24,28},{1,5},{5,9},{9,... | collective-permute-start | bytes 43208 | tf_op jit(solution)/shard_map/ppermute | solution.py:16
  63.0 7.0 %collective-permute-done.6 = f32[120,5,1,6,1]{0,4,3,2,1:T(1,128)S(1)} collective-permute-done((f32[120,5,1,6,1]{0,4,3,2,1:T(1,128)S(1)}, f32[120,5,1,6,1]{0,4,3,2,1:T(1,128)S(1)}, u32[]{:S(2)}, u32[]{:S(2)}) %collective-permute-start.6) | collective-permute-done | bytes 14432 | tf_op jit(solution)/shard_map/ppermute | solution.py:16
  79.9 4.2 %gather_fusion.3 = f32[360,4,4,128]{3,2,1,0:T(4,128)} fusion(f32[120,4,4,128]{3,2,1,0:T(4,128)S(1)} %copy.53, s32[1024]{0:T(1024)S(1)} %pad_clamp_fusion.1), kind=kCustom, calls=%fused_computation.3.clone | custom fusion | bytes 5899680 | tf_op jit(solution)/shard_map/jit(_take)/gather | solution.py:82
  84.1 4.2 %gather_fusion.2 = f32[360,4,4,128]{3,2,1,0:T(4,128)} fusion(f32[120,4,4,128]{3,2,1,0:T(4,128)S(1)} %copy.53, s32[1024]{0:T(1024)S(1)} %pad_clamp_fusion), kind=kCustom, calls=%fused_computation.1.clone | custom fusion | bytes 5899680 | tf_op jit(solution)/shard_map/jit(_take)/gather | solution.py:81
  88.7 20.5 %all_gather.3 = bf16[2,360,1,4,128]{4,1,3,2,0:T(8,128)(2,1)S(1)} all-gather(bf16[2,360,1,1,128]{4,1,3,2,0:T(8,128)(2,1)S(1)} %pad_maximum_fusion.23), channel_id=1, replica_groups=mesh['gx'=8,'gy'=8,'pa'=4] {'pa'}, dimensions={3}, use_global_device_ids=true | all-gather | bytes 921600 | tf_op jit(solution)/shard_map/all_gather | solution.py:129
  115.9 3.6 %dot_general.25 = bf16[4,4,128,360]{2,1,0,3:T(4,128)(2,1)S(1)} reshape(bf16[2048,360]{0,1:T(8,128)(2,1)} %bitcast.153) | data formatting | bytes 2949120 | tf_op jit(solution)/shard_map/dot_general | solution.py:87
  120.9 3.5 %all-to-all-start = ((bf16[120,4,1,4,128]{4,0,1,2,3:T(8,128)(2,1)}), bf16[120,4,1,4,128]{4,0,1,2,3:T(8,128)(2,1)S(1)}, u32[]{:S(2)}, u32[]{:S(2)}) async-start(bf16[120,4,1,4,128]{4,0,1,2,3:T(8,128)(2,1)} %copy.57), calls=%async_computation | async-start | bytes 983040 | tf_op jit(solution)/shard_map/all_to_all | solution.py:94
  124.3 6.2 %copy.59 = bf16[120,120,128]{1,0,2:T(8,128)(2,1)} copy(bf16[120,120,128]{2,1,0:T(8,128)(2,1)} %bitcast.159) | data formatting | bytes 7372800 | tf_op jit(solution)/shard_map/reshape.26
  130.6 6.9 %all-to-all-done = bf16[120,4,1,4,128]{4,0,1,2,3:T(8,128)(2,1)S(1)} async-done(((bf16[120,4,1,4,128]{4,0,1,2,3:T(8,128)(2,1)}), bf16[120,4,1,4,128]{4,0,1,2,3:T(8,128)(2,1)S(1)}, u32[]{:S(2)}, u32[]{:S(2)}) %all-to-all-start) | async-done | bytes 491552 | tf_op jit(solution)/shard_map/all_to_all | solution.py:94
  137.9 4.2 %convolution_bitcast_fusion.1 = f32[120,16,1,1,128]{0,1,4,3,2:T(8,128)S(1)} fusion(bf16[120,16,128]{0,1,2:T(8,128)(2,1)S(1)} %copy.58, bf16[120,120,128]{1,0,2:T(8,128)(2,1)} %copy.59), kind=kOutput, calls=%fused_computation.28 | convolution fusion | flops 58982400 | bytes 5160960 | tf_op jit(solution)/shard_map/ijlxy,jplxy->iplxy/dot_general | solution.py:95
  142.6 26.3 %all_to_all.57 = f32[120,16,1,1,128]{4,0,3,2,1:T(8,128)S(1)} all-to-all(f32[120,16,1,1,128]{4,0,3,2,1:T(8,128)S(1)} %copy.60), channel_id=1, replica_groups=mesh['gx'=8,'gy'=8,'pa'=4] {'pa'}, dimensions={1} | all-to-all | bytes 1966080 | tf_op jit(solution)/shard_map/all_to_all | solution.py:101
  169.2 4.3 %gather_fusion.5 = f32[360,4,4,128]{3,2,1,0:T(4,128)} fusion(f32[120,4,4,128]{3,2,1,0:T(4,128)S(1)} %copy.62, s32[1024]{0:T(1024)S(1)} %pad_clamp_fusion.1), kind=kCustom, calls=%fused_computation.5.clone | custom fusion | bytes 5899680 | tf_op jit(solution)/shard_map/jit(_take)/gather | solution.py:82
  173.5 4.2 %gather_fusion.4 = f32[360,4,4,128]{3,2,1,0:T(4,128)} fusion(f32[120,4,4,128]{3,2,1,0:T(4,128)S(1)} %copy.62, s32[1024]{0:T(1024)S(1)} %pad_clamp_fusion), kind=kCustom, calls=%fused_computation.4.clone | custom fusion | bytes 5899680 | tf_op jit(solution)/shard_map/jit(_take)/gather | solution.py:81
  177.7 5.5 %fusion.2 = bf16[360,4,1,4,128]{4,3,1,0,2:T(4,128)(2,1)} fusion(f32[360,4,4,128]{3,2,1,0:T(4,128)} %gather_fusion.5, f32[360,4,4,128]{3,2,1,0:T(4,128)} %gather_fusion.4, f32[360,4,128]{2,1,0:T(4,128)} %copy-done.3, f32[360,4,128]{2,1,0:T(4,128)} %copy-done.2, pred[360]{0:T(512)(128)(4,1)S(1)} %get-tuple-element.30, pred[360]{0:T(512)(128)(4,1)S(1)} %get-tuple-element.29), kind=kLoop, calls=%fused_computation.9 | loop fusion | flops 4423680 | bytes 8848080 | tf_op jit(solution)/shard_map/convert_element_type | solution.py:83
  183.2 3.7 %reshape.338 = bf16[360,2048]{1,0:T(8,128)(2,1)} reshape(bf16[360,4,1,4,128]{4,3,1,0,2:T(4,128)(2,1)} %fusion.2) | data formatting | bytes 2949120 | tf_op jit(solution)/shard_map/reshape | solution.py:88
  186.9 4.5 %dot_general.30 = bf16[4,4,128,360]{2,1,0,3:T(4,128)(2,1)} reshape(bf16[2048,360]{0,1:T(8,128)(2,1)} %bitcast.154) | data formatting | bytes 2949120 | tf_op jit(solution)/shard_map/dot_general | solution.py:87
  193.4 15.4 %all_to_all.58 = bf16[120,4,1,4,128]{4,0,1,2,3:T(8,128)(2,1)S(1)} all-to-all(bf16[120,4,1,4,128]{4,0,1,2,3:T(8,128)(2,1)S(1)} %copy.65), channel_id=1, replica_groups=mesh['gx'=8,'gy'=8,'pa'=4] {'pa'}, dimensions={3} | all-to-all | bytes 983040 | tf_op jit(solution)/shard_map/all_to_all | solution.py:94
  210.0 4.4 %convolution_bitcast_fusion = f32[120,16,1,1,128]{0,1,4,3,2:T(8,128)S(1)} fusion(bf16[120,16,128]{0,1,2:T(8,128)(2,1)} %copy.66, bf16[120,120,128]{1,0,2:T(8,128)(2,1)} %copy.59), kind=kOutput, calls=%fused_computation.27 | convolution fusion | flops 58982400 | bytes 5160960 | tf_op jit(solution)/shard_map/ijlxy,jplxy->iplxy/dot_general | solution.py:95
  215.9 27.0 %all_to_all.59 = f32[120,16,1,1,128]{4,0,3,2,1:T(8,128)S(1)} all-to-all(f32[120,16,1,1,128]{4,0,3,2,1:T(8,128)} %copy.68), channel_id=1, replica_groups=mesh['gx'=8,'gy'=8,'pa'=4] {'pa'}, dimensions={1} | all-to-all | bytes 1966080 | tf_op jit(solution)/shard_map/all_to_all | solution.py:101
  (101 shorter events, 61.8 us)
Async XLA Ops:
  2.5 5.7 %copy-start.8 = (s32[360,2]{0,1:T(2,128)S(1)}, s32[360,2]{0,1:T(2,128)}, u32[]{:S(2)}) copy-start(s32[360,2]{0,1:T(2,128)} %param.27) | copy-start | bytes 8644
  2.5 5.7 %copy-start.14 = (s32[4]{0:T(128)S(1)}, s32[4]{0:T(128)}, u32[]{:S(2)}) copy-start(s32[4]{0:T(128)} %param.32) | copy-start | bytes 52
  2.5 5.8 %copy-start.11 = (f32[1,4,128]{2,1,0:T(4,128)S(1)}, f32[1,4,128]{2,1,0:T(4,128)}, u32[]{:S(2)}) copy-start(f32[1,4,128]{2,1,0:T(4,128)} %param.23) | copy-start | bytes 6148
  2.5 5.8 %copy-start.12 = (f32[1,4,128]{2,1,0:T(4,128)S(1)}, f32[1,4,128]{2,1,0:T(4,128)}, u32[]{:S(2)}) copy-start(f32[1,4,128]{2,1,0:T(4,128)} %param.22) | copy-start | bytes 6148
  2.6 8.2 %collective-permute-start = (f32[120,5,1,1,128]{4,0,3,1,2:T(8,128)S(1)}, f32[120,5,1,1,128]{4,0,3,1,2:T(8,128)S(1)}, u32[]{:S(2)}, u32[]{:S(2)}) collective-permute-start(f32[120,5,1,1,128]{4,0,3,1,2:T(8,128)S(1)} %get-tuple-element.15), channel_id=1, source_target_pairs={{0,32},{32,64},{64,96},{96,128},{128,160},{160,192},{192,224},{1,3... | collective-permute-start | bytes 921608 | tf_op jit(solution)/shard_map/ppermute | solution.py:16
  4.5 8.0 %collective-permute-start.1 = (f32[120,5,1,1,128]{4,0,3,1,2:T(8,128)S(1)}, f32[120,5,1,1,128]{4,0,3,1,2:T(8,128)S(1)}, u32[]{:S(2)}, u32[]{:S(2)}) collective-permute-start(f32[120,5,1,1,128]{4,0,3,1,2:T(8,128)S(1)} %get-tuple-element.16), channel_id=1, source_target_pairs={{32,0},{64,32},{96,64},{128,96},{160,128},{192,160},{224,192},{33,... | collective-permute-start | bytes 921608 | tf_op jit(solution)/shard_map/ppermute | solution.py:17
  17.8 16.6 %collective-permute-start.3 = (f32[120,5,1,6,1]{0,4,3,2,1:T(1,128)S(1)}, f32[120,5,1,6,1]{0,4,3,2,1:T(1,128)S(1)}, u32[]{:S(2)}, u32[]{:S(2)}) collective-permute-start(f32[120,5,1,6,1]{0,4,3,2,1:T(1,128)S(1)} %copy.46), channel_id=1, source_target_pairs={{4,0},{8,4},{12,8},{16,12},{20,16},{24,20},{28,24},{5,1},{9,5},{13... | collective-permute-start | bytes 43208 | tf_op jit(solution)/shard_map/ppermute | solution.py:17
  20.9 11.6 %collective-permute-start.2 = (f32[120,5,1,6,1]{0,4,3,2,1:T(1,128)S(1)}, f32[120,5,1,6,1]{0,4,3,2,1:T(1,128)S(1)}, u32[]{:S(2)}, u32[]{:S(2)}) collective-permute-start(f32[120,5,1,6,1]{0,4,3,2,1:T(1,128)S(1)} %copy.44), channel_id=1, source_target_pairs={{0,4},{4,8},{8,12},{12,16},{16,20},{20,24},{24,28},{1,5},{5,9},{9,... | collective-permute-start | bytes 43208 | tf_op jit(solution)/shard_map/ppermute | solution.py:16
  34.4 1.9 copy-start.7
  39.8 5.7 %copy-start.13 = (s32[4,128]{1,0:T(4,128)S(1)}, s32[4,128]{1,0:T(4,128)}, u32[]{:S(2)}) copy-start(s32[4,128]{1,0:T(4,128)} %param.31) | copy-start | bytes 6148
  39.8 5.7 %copy-start.15 = (s32[4]{0:T(128)S(1)}, s32[4]{0:T(128)}, u32[]{:S(2)}) copy-start(s32[4]{0:T(128)} %param.33) | copy-start | bytes 52
  39.8 8.2 %collective-permute-start.4 = (f32[120,5,1,1,128]{4,0,3,1,2:T(8,128)S(1)}, f32[120,5,1,1,128]{4,0,3,1,2:T(8,128)S(1)}, u32[]{:S(2)}, u32[]{:S(2)}) collective-permute-start(f32[120,5,1,1,128]{4,0,3,1,2:T(8,128)S(1)} %get-tuple-element.13), channel_id=1, source_target_pairs={{0,32},{32,64},{64,96},{96,128},{128,160},{160,192},{192,224},{1,3... | collective-permute-start | bytes 921608 | tf_op jit(solution)/shard_map/ppermute | solution.py:16
  42.1 7.7 %collective-permute-start.5 = (f32[120,5,1,1,128]{4,0,3,1,2:T(8,128)S(1)}, f32[120,5,1,1,128]{4,0,3,1,2:T(8,128)S(1)}, u32[]{:S(2)}, u32[]{:S(2)}) collective-permute-start(f32[120,5,1,1,128]{4,0,3,1,2:T(8,128)S(1)} %get-tuple-element.14), channel_id=1, source_target_pairs={{32,0},{64,32},{96,64},{128,96},{160,128},{192,160},{224,192},{33,... | collective-permute-start | bytes 921608 | tf_op jit(solution)/shard_map/ppermute | solution.py:17
  54.3 8.7 %copy-start.10 = (f32[360]{0:T(512)S(1)}, f32[360]{0:T(512)}, u32[]{:S(2)}) copy-start(f32[360]{0:T(512)} %param.26) | copy-start | bytes 4324
  56.4 15.4 %collective-permute-start.7 = (f32[120,5,1,6,1]{0,4,3,2,1:T(1,128)S(1)}, f32[120,5,1,6,1]{0,4,3,2,1:T(1,128)S(1)}, u32[]{:S(2)}, u32[]{:S(2)}) collective-permute-start(f32[120,5,1,6,1]{0,4,3,2,1:T(1,128)S(1)} %copy.50), channel_id=1, source_target_pairs={{4,0},{8,4},{12,8},{16,12},{20,16},{24,20},{28,24},{5,1},{9,5},{13... | collective-permute-start | bytes 43208 | tf_op jit(solution)/shard_map/ppermute | solution.py:17
  58.3 11.6 %collective-permute-start.6 = (f32[120,5,1,6,1]{0,4,3,2,1:T(1,128)S(1)}, f32[120,5,1,6,1]{0,4,3,2,1:T(1,128)S(1)}, u32[]{:S(2)}, u32[]{:S(2)}) collective-permute-start(f32[120,5,1,6,1]{0,4,3,2,1:T(1,128)S(1)} %copy.48), channel_id=1, source_target_pairs={{0,4},{4,8},{8,12},{12,16},{16,20},{20,24},{24,28},{1,5},{5,9},{9,... | collective-permute-start | bytes 43208 | tf_op jit(solution)/shard_map/ppermute | solution.py:16
  84.1 4.2 %copy-start.6 = (f32[360,128]{1,0:T(8,128)S(1)}, f32[360,128]{1,0:T(8,128)}, u32[]{:S(2)}) copy-start(f32[360,128]{1,0:T(8,128)} %gather_fusion) | copy-start | bytes 552964
  84.1 4.2 %copy-start.9 = (f32[360]{0:T(512)S(1)}, f32[360]{0:T(512)}, u32[]{:S(2)}) copy-start(f32[360]{0:T(512)} %param.25) | copy-start | bytes 4324
  88.6 22.6 %copy-start.1 = (f32[360,4,4,128]{3,2,1,0:T(4,128)S(1)}, f32[360,4,4,128]{3,2,1,0:T(4,128)}, u32[]{:S(2)}) copy-start(f32[360,4,4,128]{3,2,1,0:T(4,128)} %gather_fusion.2) | copy-start | bytes 8847364
  109.3 2.2 copy-start
  115.9 3.6 %copy-start.16 = (s32[120,360]{1,0:T(8,128)S(1)}, s32[120,360]{1,0:T(8,128)}, u32[]{:S(2)}) copy-start(s32[120,360]{1,0:T(8,128)} %param.28) | copy-start | bytes 518404
  115.9 3.6 %copy-start.18 = (f32[4,128]{1,0:T(4,128)S(1)}, f32[4,128]{1,0:T(4,128)}, u32[]{:S(2)}) copy-start(f32[4,128]{1,0:T(4,128)} %param.30) | copy-start | bytes 6148
  120.9 16.6 %all-to-all-start = ((bf16[120,4,1,4,128]{4,0,1,2,3:T(8,128)(2,1)}), bf16[120,4,1,4,128]{4,0,1,2,3:T(8,128)(2,1)S(1)}, u32[]{:S(2)}, u32[]{:S(2)}) async-start(bf16[120,4,1,4,128]{4,0,1,2,3:T(8,128)(2,1)} %copy.57), calls=%async_computation | async-start | bytes 983040 | tf_op jit(solution)/shard_map/all_to_all | solution.py:94
  186.9 4.5 %copy-start.17 = (s32[120,360]{1,0:T(8,128)S(1)}, s32[120,360]{1,0:T(8,128)}, u32[]{:S(2)}) copy-start(s32[120,360]{1,0:T(8,128)} %param.28) | copy-start | bytes 518404
  (4 other events, 4.3 us)
where the time goes:
time: 246 us; the launch traced here: 244 us
  blocking collectives  89.3 us (36%)
  local copies, waits for them, and re-layouts  69.9 us (28%)
  waiting for transfers between devices  31.2 us (13%)
  starting transfers between devices  26.3 us (11%)
  other arithmetic  16.2 us (7%)
  matrix products  11.1 us (5%)
    all_to_all x2, blocking collectives, apply_inverse(): return lax.all_to_all(result, 'pa', split_axis=1, concat_axis=3, tiled=True)  53.3 us
    ppermute x4, waiting for transfers between devices, extended(): before = lax.ppermute(last, axis, up)  20.8 us
    all_gather x1, blocking collectives, shards(): lax.all_gather(coefficients(conc_rows, scratch_lines, prefactor_times_dt,...  20.5 us
    all_to_all x1, blocking collectives, apply_inverse(): lax.all_to_all(rhs_bf, 'pa', split_axis=3, concat_axis=1, tiled=True)  15.4 us
    ppermute x4, starting transfers between devices, extended(): after = lax.ppermute(initial, axis, down)  12 us
    ppermute x4, starting transfers between devices, extended(): before = lax.ppermute(last, axis, up)  10.8 us
    dot_general x2, matrix products, apply_inverse(): jnp.einsum('ijlxy,jplxy->iplxy', partition_solver_matrices, at_owner, pre...  8.64 us
    gather x2, local copies, waits for them, and re-layouts, apply_jacobian(): right_sens = jnp.take(tangent, input_compound_pair[:, 1], axis=0)  8.49 us
  transfers between devices with their start and end apart: 9, of which 7 were waited for; matrix products, arithmetic and copies ran while one was open for 4% of the time, Pallas kernels for 0%

commit v1 on v0

v1 whole, which is shorter than its diff:
```python
import functools

import jax
import jax.numpy as jnp
from jax import lax
from jax.experimental import pallas as pl
from jax.experimental.pallas import tpu as pltpu
from jax.sharding import PartitionSpec as P

NSUB = 2
LANES = 128
F32 = jnp.float32
BF16 = jnp.bfloat16
MESH = pl.DeviceIdType.MESH


def contract(a, b, dims):
    return lax.dot_general(a, b, (dims, ((), ())), preferred_element_type=F32)


def kernel(
    dims,
    sens_hbm,
    conc_hbm,
    blocks_hbm,
    temp_ref,
    u_ref,
    v_ref,
    mix_ref,
    ground_ref,
    zone_ref,
    knob_ref,
    rate_ref,
    pick_ref,
    net_ref,
    out_ref,
    sens_in,
    conc_in,
    blocks_in,
    solver,
    fields,
    stepped,
    weights,
    xs_send,
    xs_recv,
    ys_send,
    ys_recv,
    fwd_send,
    fwd_recv,
    ret_send,
    ret_recv,
    knobs,
    coef,
    flux,
    tangent,
    rhs,
    k_one,
    k_two,
    load_sem,
    knob_sems,
    xs_sems,
    xr_sems,
    ys_sems,
    yr_sems,
    fs_sems,
    fr_sems,
    rs_sems,
    rr_sems,
):
    species, reactions, groups, params, rows, x_devices, y_devices = dims
    count = params + 1
    gx, gy, me = lax.axis_index("gx"), lax.axis_index("gy"), lax.axis_index("pa")
    x_next, x_prev = lax.rem(gx + 1, x_devices), lax.rem(gx + x_devices - 1, x_devices)
    y_next, y_prev = lax.rem(gy + 1, y_devices), lax.rem(gy + y_devices - 1, y_devices)

    def peer(d):
        return lax.rem(me + d, groups)

    loads = [
        pltpu.make_async_copy(sens_hbm, sens_in, load_sem.at[0]),
        pltpu.make_async_copy(conc_hbm, conc_in, load_sem.at[1]),
        pltpu.make_async_copy(blocks_hbm, blocks_in, load_sem.at[2]),
    ]
    for load in loads:
        load.start()

    barrier = pltpu.get_barrier_semaphore()
    neighbours = [(x_prev, gy, me), (x_next, gy, me), (gx, y_prev, me), (gx, y_next, me)]
    neighbours += [(gx, gy, peer(d)) for d in range(1, groups)]
    for neighbour in neighbours:
        pl.semaphore_signal(barrier, inc=1, device_id=neighbour, device_id_type=MESH)

    lane = lax.broadcasted_iota(jnp.int32, (rows, LANES), 1)
    row = lax.broadcasted_iota(jnp.int32, (rows, LANES), 0)
    u, v, mix = u_ref[...], v_ref[...], mix_ref[...]
    u_pos, u_neg = jnp.maximum(u, 0.0), jnp.minimum(u, 0.0)
    v_pos, v_neg = jnp.maximum(v, 0.0), jnp.minimum(v, 0.0)
    from_left = jnp.where((row == 0) & (gx == 0), 0.0, u_pos + mix)
    from_right = jnp.where((row == rows - 1) & (gx == x_devices - 1), 0.0, mix - u_neg)
    from_south, from_north = v_pos + mix, mix - v_neg
    first, last = lane == 0, lane == LANES - 1
    south_edge = jnp.where(first & (gy > 0), from_south, 0.0)
    north_edge = jnp.where(last & (gy < y_devices - 1), from_north, 0.0)
    weights[0] = 1.0 - u_pos + u_neg - v_pos + v_neg - 4.0 * mix
    weights[1] = from_left
    weights[2] = from_right
    weights[3] = jnp.where(first, 0.0, from_south)
    weights[4] = jnp.where(last, 0.0, from_north)
    weights[5] = south_edge + north_edge

    tile_row = lax.broadcasted_iota(jnp.int32, (16, LANES), 0)
    tile_lane = lax.broadcasted_iota(jnp.int32, (16, LANES), 1)

    def one_hot(x, at_first, at_last):
        hit = ((tile_row == at_first + x) & (tile_lane == 0)) | (
            (tile_row == at_last + x) & (tile_lane == LANES - 1)
        )
        return jnp.where(hit, 1.0, 0.0).astype(BF16)

    gather_edge = [one_hot(x, 0, 4) for x in range(rows)]
    spread_edge = [one_hot(x, 4, 8) for x in range(rows)]

    def x_copies(sub, f):
        return [
            pltpu.make_async_remote_copy(
                src_ref=xs_send.at[sub, side, f],
                dst_ref=xs_recv.at[sub, 1 - side, f],
                send_sem=xs_sems.at[sub, side, f],
                recv_sem=xr_sems.at[sub, 1 - side, f],
                device_id=(x_prev if side == 0 else x_next, gy, me),
                device_id_type=MESH,
            )
            for side in range(2)
        ]

    def y_copies(sub, f):
        return [
            pltpu.make_async_remote_copy(
                src_ref=ys_send.at[sub, f],
                dst_ref=ys_recv.at[sub, 1 - side, f],
                send_sem=ys_sems.at[sub, side, f],
                recv_sem=yr_sems.at[sub, 1 - side, f],
                device_id=(gx, y_prev if side == 0 else y_next, me),
                device_id_type=MESH,
            )
            for side in range(2)
        ]

    def fwd_copies(c):
        return [
            pltpu.make_async_remote_copy(
                src_ref=fwd_send.at[c, peer(d)],
                dst_ref=fwd_recv.at[c, d - 1],
                send_sem=fs_sems.at[c, d - 1],
                recv_sem=fr_sems.at[c, d - 1],
                device_id=(gx, gy, peer(d)),
                device_id_type=MESH,
            )
            for d in range(1, groups)
        ]

    def ret_copies(c):
        return [
            pltpu.make_async_remote_copy(
                src_ref=ret_send.at[c, d - 1],
                dst_ref=ret_recv.at[c, d - 1],
                send_sem=rs_sems.at[c, d - 1],
                recv_sem=rr_sems.at[c, d - 1],
                device_id=(gx, gy, peer(groups - d)),
                device_id_type=MESH,
            )
            for d in range(1, groups)
        ]

    knob_copies = [
        pltpu.make_async_remote_copy(
            src_ref=knob_ref,
            dst_ref=knobs.at[d - 1],
            send_sem=knob_sems.at[0, d - 1],
            recv_sem=knob_sems.at[1, d - 1],
            device_id=(gx, gy, peer(d)),
            device_id_type=MESH,
        )
        for d in range(1, groups)
    ]

    def stage_halo(sub, f, values):
        rounded = [value.astype(BF16) for value in values]
        xs_send[sub, 0, f] = rounded[0]
        xs_send[sub, 1, f] = rounded[rows - 1]
        edge = contract(gather_edge[0], rounded[0], ((1,), (1,)))
        for x in range(1, rows):
            edge += contract(gather_edge[x], rounded[x], ((1,), (1,)))
        ys_send[sub, f, :, 0:species] = edge[0:8]

    def start_halo(sub, f):
        for copy in x_copies(sub, f) + y_copies(sub, f):
            copy.start()

    def substep(sub, f, source):
        for copy in x_copies(sub, f) + y_copies(sub, f):
            copy.wait_recv()
        beside = jnp.concatenate(
            [ys_recv[sub, 0, f, :, 0:species], ys_recv[sub, 1, f, :, 0:species]], axis=0
        ).astype(BF16)
        values = []
        for x in range(rows):
            center = source[f, x]
            left = xs_recv[sub, 0, f].astype(F32) if x == 0 else source[f, x - 1]
            right = xs_recv[sub, 1, f].astype(F32) if x == rows - 1 else source[f, x + 1]
            edge = contract(beside, spread_edge[x], ((0,), (0,)))
            w = [weights[k, x : x + 1, :] for k in range(6)]
            values.append(
                w[0] * center
                + w[1] * left
                + w[2] * right
                + w[3] * pltpu.roll(center, 1, 1)
                + w[4] * pltpu.roll(center, LANES - 1, 1)
                + w[5] * edge
            )
        return values

    def stage_input(f, held, stride, offset):
        values = []
        for x in range(rows):
            value = held[pl.ds(offset + x, species, stride=stride), :]
            fields[f, x] = value
            values.append(value)
        stage_halo(0, f, values)

    loads[0].wait()
    loads[1].wait()
    stage_input(params, conc_in, rows, 0)
    pl.semaphore_wait(barrier, len(neighbours))
    for copy in knob_copies:
        copy.start()

    @pl.loop(0, params)
    def _(f):
        stage_input(f, sens_in, params * rows, f * rows)
        start_halo(0, f)

    start_halo(0, params)

    def relayout(begin, end):
        @pl.loop(begin, end)
        def _(i):
            solver[pl.ds(i, species, stride=species), :] = blocks_in[i].astype(F32)

    loads[2].wait()
    relayout(0, species // 2)

    @pl.loop(0, count)
    def _(f):
        values = substep(0, f, fields)
        for x in range(rows):
            stepped[f, x] = values[x]
        stage_halo(1, f, values)
        start_halo(1, f)

    relayout(species // 2, species)

    @pl.loop(0, params)
    def _(f):
        values = substep(1, f, stepped)
        for x in range(rows):
            fields[f, x] = values[x]
            fwd_send[f, x] = values[x].astype(BF16)
        for copy in fwd_copies(f):
            copy.start()

    values = substep(1, params, stepped)
    for x in range(rows):
        fields[params, x] = values[x]

    conc = fields[params, me]
    conc_hi = conc.astype(BF16)
    conc_lo = (conc - conc_hi.astype(F32)).astype(BF16)
    inverse_temp = 1.0 / temp_ref[pl.ds(me, 1), :] - 1.0 / 298.0
    rate = rate_ref[0] * jnp.exp(-rate_ref[1] * inverse_temp)
    for side in range(2):
        pick = pick_ref[(1 - side) * reactions : (2 - side) * reactions, :]
        reactant = contract(pick, conc_hi, ((1,), (0,))) + contract(pick, conc_lo, ((1,), (0,)))
        coef[side] = (rate * reactant).astype(BF16).astype(F32)

    ground = ground_ref[pl.ds(me, 1), :]
    zone = zone_ref[pl.ds(me, 1), :]
    species_ids = lax.broadcasted_iota(jnp.int32, (species, LANES), 0)
    for copy in knob_copies:
        copy.wait_recv()

    def source(c, d):
        held = knob_ref if d == 0 else knobs.at[d - 1]
        hit = (species_ids == held[pl.ds(c, 1), :]) & (zone == held[pl.ds(params + c, 1), :])
        return jnp.where(hit, ground, 0.0)

    step = 128
    blocks_of_reactions = [(b, min(b + step, reactions)) for b in range(0, reactions, step)]

    def jacobian(v_bf):
        for begin, end in blocks_of_reactions:
            left = contract(pick_ref[begin:end, :], v_bf, ((1,), (0,)))
            right = contract(pick_ref[reactions + begin : reactions + end, :], v_bf, ((1,), (0,)))
            for d in range(groups):
                at = slice(d * LANES, (d + 1) * LANES)
                flux[begin:end, at] = (
                    coef[0, begin:end, :] * left[:, at] + coef[1, begin:end, :] * right[:, at]
                ).astype(BF16)
        return contract(net_ref[...], flux[...], ((1,), (0,)))

    width = 40 if species % 40 == 0 else 8

    def solve(result):
        for begin in range(0, species, width):

            def body(j, sums):
                block = solver[pl.ds(j * species + begin, width), :]
                return tuple(sums[d] + block * rhs[d, pl.ds(j, 1), :] for d in range(groups))

            zero = jnp.zeros((width, LANES), F32)
            sums = lax.fori_loop(0, species, body, (zero,) * groups, unroll=4)
            for d in range(groups):
                result[d, begin : begin + width, :] = sums[d]

    @pl.loop(0, params)
    def _(c):
        for copy in fwd_copies(c):
            copy.wait_recv()
        tiles = [fwd_send[c, me]] + [fwd_recv[c, d - 1] for d in range(1, groups)]
        tangent[...] = jnp.concatenate(tiles, axis=1)
        product = jacobian(tangent[...])
        for d in range(groups):
            rhs[d] = product[:, d * LANES : (d + 1) * LANES] + source(c, d)
        solve(k_one)
        for d in range(groups):
            at = slice(d * LANES, (d + 1) * LANES)
            tangent[:, at] = (tangent[:, at].astype(F32) + k_one[d]).astype(BF16)
        product = jacobian(tangent[...])
        for d in range(groups):
            rhs[d] = product[:, d * LANES : (d + 1) * LANES] + source(c, d) - 2.0 * k_one[d]
        solve(k_two)
        for d in range(1, groups):
            ret_send[c, d - 1] = (1.5 * k_one[d] + 0.5 * k_two[d]).astype(BF16)
        for copy in ret_copies(c):
            copy.start()
        out_ref[c, me] = fields[c, me] + 1.5 * k_one[0] + 0.5 * k_two[0]

    @pl.loop(0, params)
    def _(c):
        for copy in ret_copies(c):
            copy.wait_recv()
        for d in range(1, groups):
            x = peer(d)
            out_ref[c, x] = fields[c, x] + ret_recv[c, d - 1].astype(F32)

    for copy in knob_copies:
        copy.wait_send()

    @pl.loop(0, count)
    def _(f):
        for sub in range(NSUB):
            for copy in x_copies(sub, f) + y_copies(sub, f):
                copy.wait_send()

    @pl.loop(0, params)
    def _(c):
        for copy in fwd_copies(c) + ret_copies(c):
            copy.wait_send()


def shards(
    mixing_ratios,
    derivative_field,
    thermal_kelvin,
    eastward_cfl_ratio,
    northward_cfl_ratio,
    lateral_mixing_coef,
    prefactor_times_dt,
    barrier_kelvin,
    input_compound_pair,
    output_yield_matrix,
    partition_solver_matrices,
    ground_flux_per_tick,
    cell_zone_label,
    knob_target_compound,
    knob_zone,
):
    species, params, _, rows, lanes = derivative_field.shape
    reactions = prefactor_times_dt.shape[0]
    groups = lax.axis_size("pa")
    x_devices, y_devices = lax.axis_size("gx"), lax.axis_size("gy")
    count = params + 1

    species_ids = jnp.arange(species, dtype=jnp.int32)
    hit = input_compound_pair.T.reshape(-1)[:, None] == species_ids[None, :]
    pick = hit.astype(BF16)
    consumed = (species_ids[:, None] == input_compound_pair[None, :, 0]).astype(jnp.int32) + (
        species_ids[:, None] == input_compound_pair[None, :, 1]
    ).astype(jnp.int32)
    net = (output_yield_matrix - consumed).astype(BF16)
    rates = jnp.broadcast_to(
        jnp.stack([prefactor_times_dt, barrier_kelvin])[:, :, None], (2, reactions, lanes)
    )
    knob = jnp.broadcast_to(
        jnp.concatenate([knob_target_compound, knob_zone])[:, None], (2 * params, lanes)
    )

    vmem = pl.BlockSpec(memory_space=pltpu.VMEM)
    hbm = pl.BlockSpec(memory_space=pl.ANY)
    dma = pltpu.SemaphoreType.DMA
    tile = (species, lanes)
    moved = pl.pallas_call(
        functools.partial(
            kernel, (species, reactions, groups, params, rows, x_devices, y_devices)
        ),
        out_shape=jax.ShapeDtypeStruct((params, rows, species, lanes), F32),
        in_specs=[hbm] * 3 + [vmem] * 10,
        out_specs=vmem,
        scratch_shapes=[
            pltpu.VMEM((species * params * rows, lanes), F32),
            pltpu.VMEM((species * rows, lanes), F32),
            pltpu.VMEM((species, species, lanes), BF16),
            pltpu.VMEM((species * species, lanes), F32),
            pltpu.VMEM((count, rows) + tile, F32),
            pltpu.VMEM((count, rows) + tile, F32),
            pltpu.VMEM((6, rows, lanes), F32),
            pltpu.VMEM((NSUB, 2, count) + tile, BF16),
            pltpu.VMEM((NSUB, 2, count) + tile, BF16),
            pltpu.VMEM((NSUB, count, 8, lanes), F32),
            pltpu.VMEM((NSUB, 2, count, 8, lanes), F32),
            pltpu.VMEM((params, rows) + tile, BF16),
            pltpu.VMEM((params, groups - 1) + tile, BF16),
            pltpu.VMEM((params, groups - 1) + tile, BF16),
            pltpu.VMEM((params, groups - 1) + tile, BF16),
            pltpu.VMEM((groups - 1, 2 * params, lanes), jnp.int32),
            pltpu.VMEM((2, reactions, lanes), F32),
            pltpu.VMEM((reactions, groups * lanes), BF16),
            pltpu.VMEM((species, groups * lanes), BF16),
            pltpu.VMEM((groups,) + tile, F32),
            pltpu.VMEM((groups,) + tile, F32),
            pltpu.VMEM((groups,) + tile, F32),
            dma((3,)),
            dma((2, groups - 1)),
            dma((NSUB, 2, count)),
            dma((NSUB, 2, count)),
            dma((NSUB, 2, count)),
            dma((NSUB, 2, count)),
            dma((params, groups - 1)),
            dma((params, groups - 1)),
            dma((params, groups - 1)),
            dma((params, groups - 1)),
        ],
        compiler_params=pltpu.CompilerParams(
            collective_id=0, has_side_effects=True, vmem_limit_bytes=40 * 2**20
        ),
        name="sensitivity_step",
    )(
        derivative_field.reshape(species * params * rows, lanes),
        mixing_ratios.reshape(species * rows, lanes),
        partition_solver_matrices.reshape(species, species, lanes),
        thermal_kelvin.reshape(rows, lanes),
        eastward_cfl_ratio.reshape(rows, lanes),
        northward_cfl_ratio.reshape(rows, lanes),
        lateral_mixing_coef.reshape(rows, lanes),
        ground_flux_per_tick,
        cell_zone_label,
        knob,
        rates,
        pick,
        net,
    )
    return jnp.transpose(moved, (2, 0, 1, 3))[:, :, None]


def solution(mesh):
    in_specs = (
        P(None, None, "gx", "gy"),
        P(None, "pa", None, "gx", "gy"),
        P(None, "gx", "gy"),
        P(None, "gx", "gy"),
        P(None, "gx", "gy"),
        P(None, "gx", "gy"),
        P(),
        P(),
        P(),
        P(),
        P(None, None, None, ("gx", "pa"), "gy"),
        P("gx", "gy"),
        P("gx", "gy"),
        P("pa"),
        P("pa"),
    )
    out_specs = P(None, "pa", None, "gx", "gy")
    return jax.shard_map(shards, mesh=mesh, in_specs=in_specs, out_specs=out_specs, check_vma=False)
```

time: 246 us -> 75.7 us (0.31)
  the two profiles are of different devices: /device:TPU:130 before, /device:TPU:6 now
where the time goes in v1:
time: 75.7 us; the launch traced here: 75.2 us
  Pallas kernels  60.7 us (80%)
  local copies, waits for them, and re-layouts  12.6 us (17%)
  other arithmetic  1.9 us (3%)
    pallas_call x1, Pallas kernels, shards(): pl.pallas_call(functools.partial(kernel, (species, reactions, groups, par...  60.7 us
    unnamed x18, local copies, waits for them, and re-layouts  8.27 us

profile of v1, /device:TPU:6, one launch (start us, length us, event | category | flops | bytes accessed | tf_op | source)
XLA Modules:
  0.0 75.2 jit_solution(4940115690237018112)
XLA Ops:
  0.0 0.7 pad_add_fusion
  0.7 0.7 stack.9
  1.4 0.7 stack.10
  2.1 0.1 broadcast_in_dim.6.knob_ref
  2.2 0.8 %eq.45 = s32[720]{0:T(1024)S(1)} reshape(s32[2,360]{1,0:T(2,128)} %bitcast.19) | data formatting | bytes 5760 | tf_op jit(solution)/shard_map/eq | solution.py:395
  3.0 0.8 %slice_reduce_fusion.1 = (s32[360]{0:T(512)S(1)}, s32[360]{0:T(512)S(1)}) fusion(s32[360,2]{0,1:T(2,128)} %param.23), kind=kLoop, calls=%fused_computation.7 | loop fusion | bytes 5760 | tf_op jit(solution)/shard_map/slice | solution.py:397
  3.7 1.0 %subtract_convert_fusion.net_ref = bf16[120,360]{1,0:T(8,128)(2,1)S(1)} fusion(s32[120,360]{1,0:T(8,128)} %param.24, s32[360]{0:T(512)S(1)} %get-tuple-element.6, s32[360]{0:T(512)S(1)} %get-tuple-element.5), kind=kLoop, calls=%fused_computation.2 | loop fusion | flops 302400 | bytes 262080 | tf_op jit(solution)/shard_map/convert_element_type | solution.py:400
  4.7 0.2 fusion.pick_ref
  4.9 0.1 broadcast_in_dim.7.rate_ref
  5.0 0.0 copy-start
  5.1 2.0 %copy-done = bf16[120,120,1,1,128]{4,1,3,2,0:T(8,128)(2,1)S(1)} copy-done((bf16[120,120,1,1,128]{4,1,3,2,0:T(8,128)(2,1)S(1)}, bf16[120,120,1,1,128]{4,1,3,2,0:T(8,128)(2,1)}, u32[]{:S(2)}) %copy-start) | copy-done | bytes 3686424
  7.1 0.0 copy-start.1
  7.1 1.2 %copy-done.1 = f32[120,4,1,4,128]{4,3,2,1,0:T(4,128)S(1)} copy-done((f32[120,4,1,4,128]{4,3,2,1,0:T(4,128)S(1)}, f32[120,4,1,4,128]{4,3,2,1,0:T(4,128)}, u32[]{:S(2)}) %copy-start.1) | copy-done | bytes 983064
  8.3 0.9 %copy-done.2 = f32[120,1,4,128]{3,2,1,0:T(4,128)S(1)} copy-done((f32[120,1,4,128]{3,2,1,0:T(4,128)S(1)}, f32[120,1,4,128]{3,2,1,0:T(4,128)}, u32[]{:S(2)}) %copy-start.2) | copy-done | bytes 245784
  9.2 0.0 copy-start.3
  9.2 0.7 copy-done.3
  9.9 0.0 copy-start.4
  9.9 0.7 copy-done.4
  10.6 0.7 copy-done.5
  11.3 0.7 copy-done.6
  12.0 0.7 copy-done.7
  12.7 0.7 copy-done.8
  13.3 60.7 %sensitivity_step.1 = f32[4,4,120,128]{3,2,1,0:T(8,128)S(1)} custom-call(f32[1920,128]{1,0:T(8,128)S(1)} %bitcast.13, f32[480,128]{1,0:T(8,128)S(1)} %bitcast.14, bf16[120,120,128]{2,1,0:T(8,128)(2,1)S(1)} %bitcast.12, f32[4,128]{1,0:T(4,128)S(1)} %bitcast.15, f32[4,128]{1,0:T(4,128)S(1)} %bitcast.16, f32[4,128]{1,0:T(4,128)S(1)} %bitcast.17, ...), custom_call_target="tpu_custom_call" | custom-call | tf_op jit(solution)/shard_map/sensitivity_step/pallas_call | solution.py:412
  74.0 1.2 %copy.16 = f32[120,4,1,4,128]{4,3,2,1,0:T(4,128)} copy(f32[120,4,1,4,128]{4,0,3,1,2:T(8,128)S(1)} %bitcast.11) | data formatting | bytes 1966080 | tf_op jit(solution)/shard_map/broadcast_in_dim | solution.py:472
  (6 shorter events, 0.0 us)
Async XLA Ops:
  5.0 2.0 %copy-start = (bf16[120,120,1,1,128]{4,1,3,2,0:T(8,128)(2,1)S(1)}, bf16[120,120,1,1,128]{4,1,3,2,0:T(8,128)(2,1)}, u32[]{:S(2)}) copy-start(bf16[120,120,1,1,128]{4,1,3,2,0:T(8,128)(2,1)} %param.25) | copy-start | bytes 11059204
  7.1 1.2 %copy-start.1 = (f32[120,4,1,4,128]{4,3,2,1,0:T(4,128)S(1)}, f32[120,4,1,4,128]{4,3,2,1,0:T(4,128)}, u32[]{:S(2)}) copy-start(f32[120,4,1,4,128]{4,3,2,1,0:T(4,128)} %param.16) | copy-start | bytes 2949124
  8.3 0.9 %copy-start.2 = (f32[120,1,4,128]{3,2,1,0:T(4,128)S(1)}, f32[120,1,4,128]{3,2,1,0:T(4,128)}, u32[]{:S(2)}) copy-start(f32[120,1,4,128]{3,2,1,0:T(4,128)} %param.15) | copy-start | bytes 737284
  9.2 0.7 copy-start.3
  9.9 0.7 copy-start.4
  10.6 0.7 copy-start.5
  11.3 0.7 copy-start.6
  12.0 0.7 copy-start.7
  12.7 0.7 copy-start.8
